TPU v7x, 128 devices: a whole 4x4x4 slice. The times are simulated.
128 devices in a mesh: row: 8 (over z, core), col: 16 (over x, y).
Axes of the slice: x: 4, y: 4, z: 4, core: 2. Of those that a mesh axis runs over, the one named last changes fastest.
Arguments:
- front_panel: float32 [40960, 512], P('row', 'col'), may hold values from -16 to 48, as said below
- front_slab: float32 [40960, 8192], P('row', 'col'), may hold values from -6 to 6
- child_one: bfloat16 [8192, 8192], P('col', 'row'), may hold values from -6 to 6
- child_two: bfloat16 [8192, 8192], P('col', 'row'), may hold values from -6 to 6
- map_one: int32 [32], replicated, may hold values from 0 to 159, as said below
- map_two: int32 [32], replicated, may hold values from 0 to 159, as said below
Outputs:
- factor_panel: float32 [40960, 512], P('row', 'col')
- slab_out: float32 [40960, 8192], P('row', 'col')
Inputs may be any that keep to these rules, and one draw needn't show every extreme that they name: `front_panel`: its first 512 rows are, in all 512 columns, a symmetric positive definite block. `map_one`: distinct root row blocks. Of the 20 blocks of one index of row (numbers k * 20 to (k + 1) * 20 - 1) at most 8 are named, and exactly 8 for some index of row. `map_two`: as map_one, drawn independently.
All inputs are finite; a program needn't handle non-finite values.
Results may differ from a plain program's by a relative error of at most 0.0003.
Values may be sent and summed in bfloat16 or wider, within the bound.
A program may use at most 192 MiB of HBM per device.

v0:
```python
import jax
import jax.numpy as jnp
from jax import lax
from jax.sharding import PartitionSpec as P

P_SIZE = 256
BLK = 256


def from_root(value, axis, source):
    kept = jnp.where(lax.axis_index(axis) == source, value, 0).astype(value.dtype)
    return lax.psum(kept, axis)


def inverse_factor(block):
    lower = jnp.linalg.cholesky(block)
    identity = jnp.eye(P_SIZE, dtype=jnp.float32)
    return jax.scipy.linalg.solve_triangular(lower, identity, lower=True)


def diagonal_work(top):
    highest = lax.Precision.HIGHEST
    inverse_one = inverse_factor(top[:P_SIZE, :P_SIZE])
    first_top = jnp.dot(
        top[P_SIZE:, :P_SIZE], inverse_one.T, precision=highest, preferred_element_type=jnp.float32
    )
    second_top = top[P_SIZE:, P_SIZE:] - jnp.dot(
        first_top, first_top.T, precision=highest, preferred_element_type=jnp.float32
    )
    inverse_two = inverse_factor(second_top)
    return (inverse_one, first_top, inverse_two)


def panel_rows(panel, inverse_one, first_top, inverse_two):
    highest = lax.Precision.HIGHEST
    first_cols = jnp.dot(
        panel[:, :P_SIZE], inverse_one.T, precision=highest, preferred_element_type=jnp.float32
    )
    second_in = panel[:, P_SIZE:] - jnp.dot(
        first_cols, first_top.T, precision=highest, preferred_element_type=jnp.float32
    )
    second_cols = jnp.dot(
        second_in, inverse_two.T, precision=highest, preferred_element_type=jnp.float32
    )
    return jnp.concatenate([first_cols, second_cols], 1)


def routing(mapping, local_blocks, row_count):
    owner = mapping // local_blocks
    owner_hot = (owner[:, None] == jnp.arange(row_count, dtype=jnp.int32)[None, :]).astype(
        jnp.int32
    )
    rank = jnp.sum(owner_hot * (jnp.cumsum(owner_hot, 0) - 1), 1)
    return (owner, rank, mapping % local_blocks)


def per_device(front_panel, front_slab, child_one, child_two, map_one, map_two):
    rows_dev = front_slab.shape[0]
    slab_width = front_slab.shape[1]
    panel_width = front_panel.shape[1]
    child_blocks = map_one.shape[0]
    child_local = child_one.shape[0]
    row_count = lax.axis_size("row")
    col_count = lax.axis_size("col")
    row_rank = lax.axis_index("row")
    col_rank = lax.axis_index("col")
    piece = slab_width // row_count
    local_blocks = rows_dev // BLK
    capacity = 2 * child_blocks // row_count

    def split_columns(child):
        return child.reshape(child_local, col_count, piece)

    got_one, got_two = (
        lax.all_to_all(split_columns(child_one), "col", split_axis=1, concat_axis=0, tiled=True),
        lax.all_to_all(split_columns(child_two), "col", split_axis=1, concat_axis=0, tiled=True),
    )

    def send_rows(received, mapping):
        owner, rank, target = routing(mapping, local_blocks, row_count)
        slot = owner * capacity + rank
        select = (
            slot[None, :] == jnp.arange(row_count * capacity, dtype=jnp.int32)[:, None]
        ).astype(jnp.bfloat16)
        blocks = received.reshape(child_blocks, BLK * piece)
        packed = jnp.dot(select, blocks, preferred_element_type=jnp.float32).astype(jnp.bfloat16)
        return packed.reshape(row_count * capacity * BLK, piece)

    arrived_one, arrived_two = (
        lax.all_to_all(send_rows(got_one, map_one), "row", split_axis=0, concat_axis=1, tiled=True),
        lax.all_to_all(send_rows(got_two, map_two), "row", split_axis=0, concat_axis=1, tiled=True),
    )

    def place(arrived, mapping):
        owner, rank, target = routing(mapping, local_blocks, row_count)
        mine = (owner == row_rank)[None, :, None]
        at_block = target[None, :, None] == jnp.arange(local_blocks, dtype=jnp.int32)[:, None, None]
        at_slot = rank[None, :, None] == jnp.arange(capacity, dtype=jnp.int32)[None, None, :]
        placing = jnp.sum((at_block & at_slot & mine).astype(jnp.int32), 1).astype(jnp.bfloat16)
        added = jnp.dot(
            placing, arrived.reshape(capacity, BLK * slab_width), preferred_element_type=jnp.float32
        )
        return added.reshape(rows_dev, slab_width)

    assembled = front_slab + place(arrived_one, map_one) + place(arrived_two, map_two)
    gathered = lax.all_gather(front_panel, "col", axis=1, tiled=True)
    top = gathered[: 2 * P_SIZE]
    top = from_root(top, "row", 0)
    inverse_one, first_top, inverse_two = diagonal_work(top)
    factor = panel_rows(gathered, inverse_one, first_top, inverse_two)
    factor_out = lax.dynamic_slice_in_dim(factor, col_rank * panel_width, panel_width, 1)
    global_rows = row_rank * rows_dev + jnp.arange(rows_dev, dtype=jnp.int32)
    masked = factor * (global_rows >= 2 * P_SIZE)[:, None].astype(jnp.float32)
    wanted = (
        2 * P_SIZE
        + col_rank * slab_width
        + jnp.arange(slab_width, dtype=jnp.int32)
        - row_rank * rows_dev
    )
    valid = ((wanted >= 0) & (wanted < rows_dev))[:, None].astype(jnp.float32)
    picked = jnp.take(factor, jnp.clip(wanted, 0, rows_dev - 1), axis=0) * valid
    slab_rows = lax.psum(picked, "row")
    update = jnp.dot(
        masked, slab_rows.T, precision=lax.Precision.HIGHEST, preferred_element_type=jnp.float32
    )
    return (factor_out, assembled - update)


def solution(mesh):
    in_specs = (P("row", "col"), P("row", "col"), P("col", "row"), P("col", "row"), P(), P())
    out_specs = (P("row", "col"), P("row", "col"))
    return jax.shard_map(
        per_device, mesh=mesh, in_specs=in_specs, out_specs=out_specs, check_vma=False
    )
```

profile of v0, /device:TPU:0, one launch (start us, length us, event | category | flops | bytes accessed | tf_op | source)
XLA Modules:
  0.0 495.1 jit_solution(5786572889173300262)
XLA Ops:
  7.9 2.3 copy.39
  10.2 7.1 %all-to-all-start = ((bf16[512,16,64]{0,2,1:T(8,128)(2,1)}), bf16[512,16,64]{0,2,1:T(8,128)(2,1)S(1)}, u32[]{:S(2)}, u32[]{:S(2)}) async-start(bf16[512,16,64]{0,2,1:T(8,128)(2,1)} %bitcast.11), calls=%async_computation | async-start | bytes 2097152 | tf_op jit(solution)/shard_map/all_to_all | solution.py:75
  18.7 19.1 %all-to-all-done = bf16[512,16,64]{0,2,1:T(8,128)(2,1)S(1)} async-done(((bf16[512,16,64]{0,2,1:T(8,128)(2,1)}), bf16[512,16,64]{0,2,1:T(8,128)(2,1)S(1)}, u32[]{:S(2)}, u32[]{:S(2)}) %all-to-all-start) | async-done | bytes 1048608 | tf_op jit(solution)/shard_map/all_to_all | solution.py:75
  37.8 6.6 %all-to-all-start.2 = ((bf16[512,16,64]{0,2,1:T(8,128)(2,1)}), bf16[512,16,64]{0,2,1:T(8,128)(2,1)S(1)}, u32[]{:S(2)}, u32[]{:S(2)}) async-start(bf16[512,16,64]{0,2,1:T(8,128)(2,1)} %bitcast.15), calls=%async_computation.2 | async-start | bytes 2097152 | tf_op jit(solution)/shard_map/all_to_all | solution.py:76
  44.8 2.0 copy.40
  46.8 2.5 reshape.193
  49.3 1.9 convolution_convert_fusion.1
  51.2 5.5 %all_to_all.49 = bf16[8,2048,64]{2,1,0:T(8,128)(2,1)} reshape(bf16[64,16384]{1,0:T(8,128)(2,1)S(1)} %convolution_convert_fusion.1) | data formatting | bytes 4194304 | tf_op jit(solution)/shard_map/all_to_all | solution.py:90
  56.7 4.8 copy.41
  61.5 6.5 %all-to-all-start.1 = ((bf16[8,2048,64]{1,2,0:T(8,128)(2,1)}), bf16[8,2048,64]{1,2,0:T(8,128)(2,1)S(1)}, u32[]{:S(2)}, u32[]{:S(2)}) async-start(bf16[8,2048,64]{1,2,0:T(8,128)(2,1)} %copy.41), calls=%async_computation.1 | async-start | bytes 4194304 | tf_op jit(solution)/shard_map/all_to_all | solution.py:90
  68.4 1.8 copy.44
  70.2 2.8 reshape.197
  73.1 2.0 convolution_convert_fusion
  75.1 6.5 %all_to_all.55 = bf16[8,2048,64]{2,1,0:T(8,128)(2,1)} reshape(bf16[64,16384]{1,0:T(8,128)(2,1)} %convolution_convert_fusion) | data formatting | bytes 4194304 | tf_op jit(solution)/shard_map/all_to_all | solution.py:91
  81.6 4.8 copy.45
  86.4 8.9 %all-to-all-done.1 = bf16[8,2048,64]{1,2,0:T(8,128)(2,1)S(1)} async-done(((bf16[8,2048,64]{1,2,0:T(8,128)(2,1)}), bf16[8,2048,64]{1,2,0:T(8,128)(2,1)S(1)}, u32[]{:S(2)}, u32[]{:S(2)}) %all-to-all-start.1) | async-done | bytes 2097184 | tf_op jit(solution)/shard_map/all_to_all | solution.py:90
  95.2 4.3 all-to-all-start.3
  100.8 4.2 copy.42
  105.0 5.0 %reshape.232 = bf16[1048576]{0:T(1024)(128)(2,1)S(1)} reshape(bf16[2048,8,64]{2,1,0:T(8,128)(2,1)} %copy.42) | data formatting | bytes 4194304
  110.1 2.2 reshape.194
  112.3 7.9 %fusion.38 = f32[20,131072]{1,0:T(8,128)} fusion(bf16[8,131072]{1,0:T(8,128)(2,1)} %reshape.194, s32[20,8]{1,0:T(8,128)S(1)} %convert_reduce_fusion.1), kind=kOutput, calls=%fused_computation.86 | convolution fusion | flops 41943200 | bytes 12583552 | tf_op jit(solution)/shard_map/dot_general | solution.py:100
  120.2 10.5 %reshape.195 = f32[5120,512]{1,0:T(8,128)} reshape(f32[20,131072]{1,0:T(8,128)} %fusion.38) | data formatting | bytes 20971520 | tf_op jit(solution)/shard_map/reshape | solution.py:103
  130.7 5.6 %copy.46 = bf16[2048,8,64]{2,1,0:T(8,128)(2,1)} copy(bf16[2048,8,64]{0,2,1:T(8,128)(2,1)} %bitcast.18) | data formatting | bytes 4194304 | tf_op jit(solution)/shard_map/all_to_all | solution.py:91
  136.4 5.0 %reshape.230 = bf16[1048576]{0:T(1024)(128)(2,1)S(1)} reshape(bf16[2048,8,64]{2,1,0:T(8,128)(2,1)} %copy.46) | data formatting | bytes 4194304
  141.4 2.2 reshape.198
  143.6 2.3 slice_select_fusion
  146.0 7.9 %fusion.36 = f32[20,131072]{1,0:T(8,128)} fusion(bf16[8,131072]{1,0:T(8,128)(2,1)} %reshape.198, s32[20,8]{1,0:T(8,128)S(1)} %convert_reduce_fusion), kind=kOutput, calls=%fused_computation.84 | convolution fusion | flops 41943200 | bytes 12583552 | tf_op jit(solution)/shard_map/dot_general | solution.py:100
  153.9 11.0 %reshape.199 = f32[5120,512]{1,0:T(8,128)} reshape(f32[20,131072]{1,0:T(8,128)} %fusion.36) | data formatting | bytes 20971520 | tf_op jit(solution)/shard_map/reshape | solution.py:103
  164.9 45.9 %all-reduce.4.cloned.1.call-done = f32[512,512]{0,1:T(8,128)} async-done(((f32[512,512]{0,1:T(8,128)}), f32[512,512]{0,1:T(8,128)}) %all-reduce.4.cloned.1.call-update) | async-done | bytes 1048592 | tf_op jit(solution)/shard_map/psum | solution.py:12
  213.1 11.7 %cholesky.130 = f32[128,128]{1,0:T(8,128)S(1)} custom-call(f32[128,128]{1,0:T(8,128)S(1)} %cholesky.194), custom_call_target="Cholesky" | custom-call | tf_op jit(solution)/shard_map/jit(cholesky)/cholesky | solution.py:16
  224.8 9.8 %custom-call.13 = f32[1,128,128]{1,2,0:T(8,128)S(1)} custom-call(f32[1,128,128]{2,1,0:T(8,128)S(1)} %get-tuple-element.51), custom_call_target="InvertDiagBlocksLowerTriangular" | custom-call | tf_op jit(solution)/shard_map/jit(cholesky)/cholesky | solution.py:16
  235.1 11.7 %cholesky.147 = f32[128,128]{1,0:T(8,128)S(1)} custom-call(f32[128,128]{1,0:T(8,128)S(1)} %convolution_subtract_fusion.5), custom_call_target="Cholesky" | custom-call | tf_op jit(solution)/shard_map/jit(cholesky)/cholesky | solution.py:16
  248.9 3.9 while.4
  252.8 19.8 %custom-call.14 = f32[2,128,128]{1,2,0:T(8,128)S(1)} custom-call(f32[2,128,128]{2,1,0:T(8,128)S(1)} %get-tuple-element.18), custom_call_target="InvertDiagBlocksLowerTriangular" | custom-call | tf_op jit(solution)/shard_map/jit(_solve_triangular)/triangular_solve | solution.py:18
  274.8 11.7 %cholesky.164 = f32[128,128]{1,0:T(8,128)S(1)} custom-call(f32[128,128]{1,0:T(8,128)S(1)} %cholesky.197), custom_call_target="Cholesky" | custom-call | tf_op jit(solution)/shard_map/jit(cholesky)/cholesky | solution.py:16
  286.5 9.8 %custom-call.15 = f32[1,128,128]{1,2,0:T(8,128)S(1)} custom-call(f32[1,128,128]{2,1,0:T(8,128)S(1)} %get-tuple-element.47), custom_call_target="InvertDiagBlocksLowerTriangular" | custom-call | tf_op jit(solution)/shard_map/jit(cholesky)/cholesky | solution.py:16
  296.8 11.7 %cholesky.181 = f32[128,128]{1,0:T(8,128)S(1)} custom-call(f32[128,128]{1,0:T(8,128)S(1)} %convolution_subtract_fusion.4), custom_call_target="Cholesky" | custom-call | tf_op jit(solution)/shard_map/jit(cholesky)/cholesky | solution.py:16
  311.3 4.1 while.5
  315.4 19.9 %custom-call.16 = f32[2,128,128]{1,2,0:T(8,128)S(1)} custom-call(f32[2,128,128]{2,1,0:T(8,128)S(1)} %get-tuple-element.19), custom_call_target="InvertDiagBlocksLowerTriangular" | custom-call | tf_op jit(solution)/shard_map/jit(_solve_triangular)/triangular_solve | solution.py:18
  336.2 6.7 %fusion.4 = f32[256,5120]{1,0:T(8,128)S(1)} fusion(f32[5120,512]{0,1:T(8,128)} %all-gather.2.cloned.1.call-done, f32[128,256]{1,0:T(8,128)S(1)} %fusion.26, f32[128,256]{1,0:T(8,128)S(1)} %fusion.19), kind=kOutput, calls=%fused_computation.14 | convolution fusion | flops 4026597376 | bytes 10747904 | tf_op jit(solution)/shard_map/dot_general | solution.py:36
  342.9 9.0 %convolution_subtract_fusion = f32[5120,256]{0,1:T(8,128)S(1)} fusion(f32[256,5120]{1,0:T(8,128)S(1)} %fusion.4, f32[256,256]{1,0:T(8,128)S(1)} %fusion.8, f32[5120,512]{0,1:T(8,128)} %all-gather.2.cloned.1.call-done), kind=kOutput, calls=%fused_computation.13 | convolution fusion | flops 4027842560 | bytes 15990784 | tf_op jit(solution)/shard_map/dot_general | solution.py:39
  351.9 6.5 %fusion.10 = f32[5120,256]{0,1:T(8,128)} fusion(f32[5120,256]{0,1:T(8,128)S(1)} %convolution_subtract_fusion, f32[128,256]{1,0:T(8,128)S(1)} %fusion.22, f32[128,256]{1,0:T(8,128)S(1)} %fusion.17), kind=kOutput, calls=%fused_computation.30 | convolution fusion | flops 4026597376 | bytes 10747904 | tf_op jit(solution)/shard_map/dot_general | solution.py:42
  358.4 9.3 %pad_maximum_fusion = f32[5120,512]{0,1:T(8,128)} fusion(f32[5120,256]{0,1:T(8,128)} %fusion.10, f32[5120,256]{0,1:T(8,128)} %bitcast.92), kind=kLoop, calls=%fused_computation.8 | loop fusion | flops 2621440 | bytes 20971520 | tf_op jit(solution)/shard_map/concatenate | solution.py:45
  367.7 11.4 %copy.47 = f32[5120,512]{1,0:T(8,128)} copy(f32[5120,512]{0,1:T(8,128)} %pad_maximum_fusion) | data formatting | bytes 20971520 | tf_op jit(solution)/shard_map/concatenate | solution.py:45
  379.1 6.2 %gather_fusion = f32[512,512]{1,0:T(8,128)S(1)} fusion(f32[5120,512]{1,0:T(8,128)} %copy.47, s32[1024]{0:T(1024)S(1)} %pad_clamp_fusion), kind=kCustom, calls=%fused_computation | custom fusion | bytes 2099200 | tf_op jit(solution)/shard_map/jit(_take)/gather | solution.py:121
  386.6 2.0 fusion.7
  388.6 60.0 %all-reduce.6.cloned.1.call-done = f32[512,512]{1,0:T(8,128)} async-done(((f32[512,512]{1,0:T(8,128)}), f32[512,512]{1,0:T(8,128)}) %all-reduce.6.cloned.1.call-update) | async-done | bytes 1048592 | tf_op jit(solution)/shard_map/psum | solution.py:122
  448.6 39.6 %add_subtract_fusion = f32[5120,512]{1,0:T(8,128)} fusion(f32[5120,512]{1,0:T(8,128)} %reshape.199, f32[5120,512]{1,0:T(8,128)} %param.10, f32[5120,512]{1,0:T(8,128)} %reshape.195, f32[512,512]{1,0:T(8,128)} %all-reduce.6.cloned.1.call-done, f32[5120]{0:T(1024)S(1)} %fusion.31, f32[5120,256]{0,1:T(8,128)} %fusion.10, f32[5120,256]{0,1:T(8,128)} %bitcast.94), kind=kOutput, calls=%fused_computation.12 | convolution fusion | flops 16119234560 | bytes 53497856 | tf_op jit(solution)/shard_map/dot_general | solution.py:123
  (90 shorter events, 21.5 us)
Async XLA Ops:
  7.2 10.2 %copy-start.3 = (bf16[512,1024]{1,0:T(8,128)(2,1)S(1)}, bf16[512,1024]{1,0:T(8,128)(2,1)}, u32[]{:S(2)}) copy-start(bf16[512,1024]{1,0:T(8,128)(2,1)} %param.12) | copy-start | bytes 3145732
  7.2 37.2 %copy-start.5 = (s32[32]{0:T(128)S(1)}, s32[32]{0:T(128)}, u32[]{:S(2)}) copy-start(s32[32]{0:T(128)} %param.13) | copy-start | bytes 388
  7.2 37.2 %copy-start.4 = (s32[32]{0:T(128)S(1)}, s32[32]{0:T(128)}, u32[]{:S(2)}) copy-start(s32[32]{0:T(128)} %param.14) | copy-start | bytes 388
  7.2 136.4 %all-gather.2.cloned.1.call-start = ((), (), s32[]{:S(2)}) async-start(), calls=%async_computation.4 | async-start | bytes 11141120 | tf_op jit(solution)/shard_map/all_gather | solution.py:106
  10.2 27.6 %all-to-all-start = ((bf16[512,16,64]{0,2,1:T(8,128)(2,1)}), bf16[512,16,64]{0,2,1:T(8,128)(2,1)S(1)}, u32[]{:S(2)}, u32[]{:S(2)}) async-start(bf16[512,16,64]{0,2,1:T(8,128)(2,1)} %bitcast.11), calls=%async_computation | async-start | bytes 2097152 | tf_op jit(solution)/shard_map/all_to_all | solution.py:75
  37.8 7.0 %copy-start.1 = (bf16[512,16,64]{0,2,1:T(8,128)(2,1)}, bf16[512,16,64]{0,2,1:T(8,128)(2,1)S(1)}, u32[]{:S(2)}) copy-start(bf16[512,16,64]{0,2,1:T(8,128)(2,1)S(1)} %all-to-all-done) | copy-start | bytes 3145732
  37.8 23.7 %all-to-all-start.2 = ((bf16[512,16,64]{0,2,1:T(8,128)(2,1)}), bf16[512,16,64]{0,2,1:T(8,128)(2,1)S(1)}, u32[]{:S(2)}, u32[]{:S(2)}) async-start(bf16[512,16,64]{0,2,1:T(8,128)(2,1)} %bitcast.15), calls=%async_computation.2 | async-start | bytes 2097152 | tf_op jit(solution)/shard_map/all_to_all | solution.py:76
  61.5 33.7 %all-to-all-start.1 = ((bf16[8,2048,64]{1,2,0:T(8,128)(2,1)}), bf16[8,2048,64]{1,2,0:T(8,128)(2,1)S(1)}, u32[]{:S(2)}, u32[]{:S(2)}) async-start(bf16[8,2048,64]{1,2,0:T(8,128)(2,1)} %copy.41), calls=%async_computation.1 | async-start | bytes 4194304 | tf_op jit(solution)/shard_map/all_to_all | solution.py:90
  95.2 35.5 %all-to-all-start.3 = ((bf16[8,2048,64]{1,2,0:T(8,128)(2,1)}), bf16[8,2048,64]{1,2,0:T(8,128)(2,1)}, u32[]{:S(2)}, u32[]{:S(2)}) async-start(bf16[8,2048,64]{1,2,0:T(8,128)(2,1)} %copy.45), calls=%async_computation.3 | async-start | bytes 4194304 | tf_op jit(solution)/shard_map/all_to_all | solution.py:91
  99.6 111.3 %all-reduce.4.cloned.1.call-start = ((), (), s32[]{:S(2)}) async-start(), calls=%async_computation.5 | async-start | bytes 2097152 | tf_op jit(solution)/shard_map/psum | solution.py:12
  146.0 302.6 %all-reduce.6.cloned.1.call-start = ((), (), s32[]{:S(2)}) async-start(), calls=%async_computation.6 | async-start | bytes 2097152 | tf_op jit(solution)/shard_map/psum | solution.py:122
  210.9 62.7 %copy-start.2 = (f32[512,512]{0,1:T(8,128)S(1)}, f32[512,512]{0,1:T(8,128)}, u32[]{:S(2)}) copy-start(f32[512,512]{0,1:T(8,128)} %all-reduce.4.cloned.1.call-done) | copy-start | bytes 3145732
  342.9 9.0 %copy-start = (f32[256,5120]{1,0:T(8,128)}, f32[256,5120]{1,0:T(8,128)S(1)}, u32[]{:S(2)}) copy-start(f32[256,5120]{1,0:T(8,128)S(1)} %fusion.4) | copy-start | bytes 15728644
Sparse Core Ops, SparseCore 0:
  10.2 89.2 all-gather.1
  146.1 64.7 all-reduce.3
  386.7 61.7 all-reduce.5
where the time goes:
time: 502 us; the launch traced here: 495 us
  waiting for transfers between devices  135 us (27%)
  other arithmetic  126 us (25%)
  local copies, waits for them, and re-layouts  107 us (21%)
  matrix products  85.3 us (17%)
  starting transfers between devices  24.9 us (5%)
  between operations  17.2 us (3%)
    another operation x13, other arithmetic, inverse_factor(): lower = jnp.linalg.cholesky(block)  68.6 us
    psum x1, waiting for transfers between devices, per_device(): slab_rows = lax.psum(picked, 'row')  60 us
    psum x1, waiting for transfers between devices, from_root(): return lax.psum(kept, axis)  45.9 us
    another operation x5, other arithmetic, inverse_factor(): return jax.scipy.linalg.solve_triangular(lower, identity, lower=True)  39.8 us
    dot_general x1, matrix products, per_device(): jnp.dot(masked, slab_rows.T, precision=lax.Precision.HIGHEST, preferred_e...  39.6 us
    reshape x2, local copies, waits for them, and re-layouts, place(): return added.reshape(rows_dev, slab_width)  21.5 us
    all_to_all x1, waiting for transfers between devices, per_device(): lax.all_to_all(split_columns(child_one), 'col', split_axis=1, concat_axis...  19.1 us
    all_to_all x3, local copies, waits for them, and re-layouts, per_device(): lax.all_to_all(send_rows(got_two, map_two), 'row', split_axis=0, concat_a...  16.9 us
  transfers between devices with their start and end apart: 7, of which 4 were waited for; matrix products, arithmetic and copies ran while one was open for 18% of the time, Pallas kernels for 0%

commit v1 on v0

--- a/solution.py
+++ b/solution.py
@@ -7,9 +7,15 @@
 BLK = 256
 
 
+def gather_and_add(shard, mesh_axis):
+    parts = lax.all_gather(shard, mesh_axis, axis=0, tiled=False)
+    total = parts.sum(axis=0)
+    return total
+
+
 def from_root(value, axis, source):
     kept = jnp.where(lax.axis_index(axis) == source, value, 0).astype(value.dtype)
-    return lax.psum(kept, axis)
+    return gather_and_add(kept, axis)
 
 
 def inverse_factor(block):

time: 502 us -> 558 us (1.11)
  waiting for transfers between devices: 135 us -> 173 us
  local copies, waits for them, and re-layouts: 107 us -> 127 us
  starting transfers between devices: 24.9 us -> 17.9 us
    all_gather x1, waiting for transfers between devices: 0.01 us -> 85 us  [per_device(): gathered = lax.all_gather(front_panel, 'col', axis=1, tiled=True)]
    psum x1 -> x0, waiting for transfers between devices: 45.9 us -> none  [from_root(): return lax.psum(kept, axis)]
    all_gather x0 -> x1, local copies, waits for them, and re-layouts: none -> 9 us  [gather_and_add(): parts = lax.all_gather(shard, mesh_axis, axis=0, tiled=False)]
    unnamed x16 -> x21, local copies, waits for them, and re-layouts: 13.7 us -> 20.1 us
  transfers between devices with their start and end apart: 7 -> 7, of which waited for: 4 -> 4; matrix products, arithmetic and copies ran while one was open for 18% -> 19% of each run, Pallas kernels for 0% -> 0%
where the time goes in v1:
time: 558 us; the launch traced here: 550 us
  waiting for transfers between devices  173 us (31%)
  other arithmetic  130 us (23%)
  local copies, waits for them, and re-layouts  127 us (23%)
  matrix products  85.3 us (15%)
  starting transfers between devices  17.9 us (3%)
  between operations  17 us (3%)
    all_gather x1, waiting for transfers between devices, per_device(): gathered = lax.all_gather(front_panel, 'col', axis=1, tiled=True)  85 us
    another operation x13, other arithmetic, inverse_factor(): lower = jnp.linalg.cholesky(block)  68.7 us
    psum x1, waiting for transfers between devices, per_device(): slab_rows = lax.psum(picked, 'row')  62.6 us
    another operation x5, other arithmetic, inverse_factor(): return jax.scipy.linalg.solve_triangular(lower, identity, lower=True)  40 us
    dot_general x1, matrix products, per_device(): jnp.dot(masked, slab_rows.T, precision=lax.Precision.HIGHEST, preferred_e...  39.6 us
    reshape x2, local copies, waits for them, and re-layouts, place(): return added.reshape(rows_dev, slab_width)  21.1 us
    unnamed x21, local copies, waits for them, and re-layouts  20.1 us
    all_to_all x3, local copies, waits for them, and re-layouts, per_device(): lax.all_to_all(send_rows(got_two, map_two), 'row', split_axis=0, concat_a...  16.9 us
  transfers between devices with their start and end apart: 7, of which 4 were waited for; matrix products, arithmetic and copies ran while one was open for 19% of the time, Pallas kernels for 0%

profile of v1, /device:TPU:0, one launch (start us, length us, event | category | flops | bytes accessed | tf_op | source)
XLA Modules:
  0.0 550.3 jit_solution(14118535015445356019)
XLA Ops:
  8.0 85.0 %all-gather.4.cloned.1.call-done = f32[5120,512]{0,1:T(8,128)} async-done(((f32[5120,32]{0,1:T(8,128)}), f32[5120,512]{0,1:T(8,128)}) %all-gather.4.cloned.1.call-update) | async-done | bytes 10485776 | tf_op jit(solution)/shard_map/all_gather | solution.py:112
  93.0 2.3 slice_select_fusion
  95.3 2.3 copy.58
  97.6 5.3 all-to-all-start
  104.2 16.4 %all-to-all-done = bf16[512,16,64]{0,2,1:T(8,128)(2,1)S(1)} async-done(((bf16[512,16,64]{0,2,1:T(8,128)(2,1)}), bf16[512,16,64]{0,2,1:T(8,128)(2,1)S(1)}, u32[]{:S(2)}, u32[]{:S(2)}) %all-to-all-start) | async-done | bytes 1048608 | tf_op jit(solution)/shard_map/all_to_all | solution.py:81
  120.6 3.7 all-to-all-start.2
  126.6 2.5 reshape.193
  131.0 5.5 %all_to_all.49 = bf16[8,2048,64]{2,1,0:T(8,128)(2,1)} reshape(bf16[64,16384]{1,0:T(8,128)(2,1)S(1)} %convolution_convert_fusion.1) | data formatting | bytes 4194304 | tf_op jit(solution)/shard_map/all_to_all | solution.py:96
  136.6 4.8 copy.60
  141.4 4.5 all-to-all-start.1
  148.0 2.8 reshape.197
  150.9 2.1 convolution_convert_fusion
  152.9 6.5 %all_to_all.55 = bf16[8,2048,64]{2,1,0:T(8,128)(2,1)} reshape(bf16[64,16384]{1,0:T(8,128)(2,1)} %convolution_convert_fusion) | data formatting | bytes 4194304 | tf_op jit(solution)/shard_map/all_to_all | solution.py:97
  159.4 4.8 copy.64
  164.2 8.8 %all-to-all-done.1 = bf16[8,2048,64]{1,2,0:T(8,128)(2,1)S(1)} async-done(((bf16[8,2048,64]{1,2,0:T(8,128)(2,1)}), bf16[8,2048,64]{1,2,0:T(8,128)(2,1)S(1)}, u32[]{:S(2)}, u32[]{:S(2)}) %all-to-all-start.1) | async-done | bytes 2097184 | tf_op jit(solution)/shard_map/all_to_all | solution.py:96
  173.0 4.4 all-to-all-start.3
  178.4 4.7 copy.61
  183.1 5.0 reshape.233
  188.1 2.2 reshape.194
  190.3 7.9 %fusion.38 = f32[20,131072]{1,0:T(8,128)} fusion(bf16[8,131072]{1,0:T(8,128)(2,1)} %reshape.194, s32[20,8]{1,0:T(8,128)S(1)} %convert_reduce_fusion.1), kind=kOutput, calls=%fused_computation.86 | convolution fusion | flops 41943200 | bytes 12583552 | tf_op jit(solution)/shard_map/dot_general | solution.py:106
  198.2 10.5 %reshape.195 = f32[5120,512]{1,0:T(8,128)} reshape(f32[20,131072]{1,0:T(8,128)} %fusion.38) | data formatting | bytes 20971520 | tf_op jit(solution)/shard_map/reshape | solution.py:109
  208.8 5.6 %copy.65 = bf16[2048,8,64]{2,1,0:T(8,128)(2,1)} copy(bf16[2048,8,64]{0,2,1:T(8,128)(2,1)} %bitcast.19) | data formatting | bytes 4194304 | tf_op jit(solution)/shard_map/all_to_all | solution.py:97
  214.4 5.0 reshape.231
  219.5 2.2 reshape.198
  221.7 7.9 %fusion.36 = f32[20,131072]{1,0:T(8,128)} fusion(bf16[8,131072]{1,0:T(8,128)(2,1)} %reshape.198, s32[20,8]{1,0:T(8,128)S(1)} %convert_reduce_fusion), kind=kOutput, calls=%fused_computation.84 | convolution fusion | flops 41943200 | bytes 12583552 | tf_op jit(solution)/shard_map/dot_general | solution.py:106
  229.6 10.5 %reshape.199 = f32[5120,512]{1,0:T(8,128)} reshape(f32[20,131072]{1,0:T(8,128)} %fusion.36) | data formatting | bytes 20971520 | tf_op jit(solution)/shard_map/reshape | solution.py:109
  240.1 5.4 slice.75
  245.5 6.1 %copy.70 = f32[5120,256]{1,0:T(8,128)} copy(f32[5120,256]{0,1:T(8,128)} %slice.75) | data formatting | bytes 10485760
  251.6 9.0 %copy.68 = f32[4096,512]{1,0:T(8,128)} copy(f32[4096,512]{0,1:T(8,128)} %all-gather.6.cloned.1.call-done) | data formatting | bytes 16777216 | tf_op jit(solution)/shard_map/all_gather | solution.py:11
  260.6 4.5 reduce_sum.43
  265.3 11.7 %cholesky.130 = f32[128,128]{1,0:T(8,128)S(1)} custom-call(f32[128,128]{1,0:T(8,128)S(1)} %cholesky.194), custom_call_target="Cholesky" | custom-call | tf_op jit(solution)/shard_map/jit(cholesky)/cholesky | solution.py:22
  277.1 9.8 %custom-call.13 = f32[1,128,128]{1,2,0:T(8,128)S(1)} custom-call(f32[1,128,128]{2,1,0:T(8,128)S(1)} %get-tuple-element.53), custom_call_target="InvertDiagBlocksLowerTriangular" | custom-call | tf_op jit(solution)/shard_map/jit(cholesky)/cholesky | solution.py:22
  287.4 11.7 %cholesky.147 = f32[128,128]{1,0:T(8,128)S(1)} custom-call(f32[128,128]{1,0:T(8,128)S(1)} %convolution_subtract_fusion.5), custom_call_target="Cholesky" | custom-call | tf_op jit(solution)/shard_map/jit(cholesky)/cholesky | solution.py:22
  301.2 4.1 while.4
  305.3 20.1 %custom-call.14 = f32[2,128,128]{1,2,0:T(8,128)S(1)} custom-call(f32[2,128,128]{2,1,0:T(8,128)S(1)} %get-tuple-element.18), custom_call_target="InvertDiagBlocksLowerTriangular" | custom-call | tf_op jit(solution)/shard_map/jit(_solve_triangular)/triangular_solve | solution.py:24
  327.5 11.7 %cholesky.164 = f32[128,128]{1,0:T(8,128)S(1)} custom-call(f32[128,128]{1,0:T(8,128)S(1)} %cholesky.197), custom_call_target="Cholesky" | custom-call | tf_op jit(solution)/shard_map/jit(cholesky)/cholesky | solution.py:22
  339.2 9.8 %custom-call.15 = f32[1,128,128]{1,2,0:T(8,128)S(1)} custom-call(f32[1,128,128]{2,1,0:T(8,128)S(1)} %get-tuple-element.49), custom_call_target="InvertDiagBlocksLowerTriangular" | custom-call | tf_op jit(solution)/shard_map/jit(cholesky)/cholesky | solution.py:22
  349.5 11.7 %cholesky.181 = f32[128,128]{1,0:T(8,128)S(1)} custom-call(f32[128,128]{1,0:T(8,128)S(1)} %convolution_subtract_fusion.4), custom_call_target="Cholesky" | custom-call | tf_op jit(solution)/shard_map/jit(cholesky)/cholesky | solution.py:22
  364.0 4.0 while.5
  367.9 19.8 %custom-call.16 = f32[2,128,128]{1,2,0:T(8,128)S(1)} custom-call(f32[2,128,128]{2,1,0:T(8,128)S(1)} %get-tuple-element.19), custom_call_target="InvertDiagBlocksLowerTriangular" | custom-call | tf_op jit(solution)/shard_map/jit(_solve_triangular)/triangular_solve | solution.py:24
  388.7 7.0 %fusion.4 = f32[256,5120]{1,0:T(8,128)S(1)} fusion(f32[5120,512]{0,1:T(8,128)} %all-gather.4.cloned.1.call-done, f32[128,256]{1,0:T(8,128)S(1)} %fusion.26, f32[128,256]{1,0:T(8,128)S(1)} %fusion.19), kind=kOutput, calls=%fused_computation.14 | convolution fusion | flops 4026597376 | bytes 10747904 | tf_op jit(solution)/shard_map/dot_general | solution.py:42
  395.7 8.9 %convolution_subtract_fusion = f32[5120,256]{1,0:T(8,128)S(1)} fusion(f32[5120,256]{1,0:T(8,128)S(1)} %bitcast.98, f32[256,5120]{1,0:T(8,128)S(1)} %fusion.4, f32[256,256]{1,0:T(8,128)S(1)} %fusion.8), kind=kOutput, calls=%fused_computation.13 | convolution fusion | flops 4027842560 | bytes 15990784 | tf_op jit(solution)/shard_map/dot_general | solution.py:45
  404.6 6.5 %fusion.10 = f32[5120,256]{0,1:T(8,128)} fusion(f32[5120,256]{1,0:T(8,128)S(1)} %convolution_subtract_fusion, f32[128,256]{1,0:T(8,128)S(1)} %fusion.22, f32[128,256]{1,0:T(8,128)S(1)} %fusion.17), kind=kOutput, calls=%fused_computation.30 | convolution fusion | flops 4026597376 | bytes 10747904 | tf_op jit(solution)/shard_map/dot_general | solution.py:48
  411.1 9.3 %pad_maximum_fusion = f32[5120,512]{0,1:T(8,128)} fusion(f32[5120,256]{0,1:T(8,128)} %fusion.10, f32[5120,256]{0,1:T(8,128)} %bitcast.93), kind=kLoop, calls=%fused_computation.8 | loop fusion | flops 2621440 | bytes 20971520 | tf_op jit(solution)/shard_map/concatenate | solution.py:51
  420.4 11.4 %copy.66 = f32[5120,512]{1,0:T(8,128)} copy(f32[5120,512]{0,1:T(8,128)} %pad_maximum_fusion) | data formatting | bytes 20971520 | tf_op jit(solution)/shard_map/concatenate | solution.py:51
  431.8 6.2 %gather_fusion = f32[512,512]{1,0:T(8,128)S(1)} fusion(f32[5120,512]{1,0:T(8,128)} %copy.66, s32[1024]{0:T(1024)S(1)} %pad_clamp_fusion), kind=kCustom, calls=%fused_computation | custom fusion | bytes 2099200 | tf_op jit(solution)/shard_map/jit(_take)/gather | solution.py:127
  441.3 62.6 %all-reduce.3.cloned.1.call-done = f32[512,512]{1,0:T(8,128)} async-done(((f32[512,512]{1,0:T(8,128)}), f32[512,512]{1,0:T(8,128)}) %all-reduce.3.cloned.1.call-update) | async-done | bytes 1048592 | tf_op jit(solution)/shard_map/psum | solution.py:128
  503.9 39.6 %add_subtract_fusion = f32[5120,512]{1,0:T(8,128)} fusion(f32[5120,512]{1,0:T(8,128)} %reshape.199, f32[5120,512]{1,0:T(8,128)} %param.10, f32[5120,512]{1,0:T(8,128)} %reshape.195, f32[512,512]{1,0:T(8,128)} %all-reduce.3.cloned.1.call-done, f32[5120]{0:T(1024)S(1)} %fusion.31, f32[5120,256]{0,1:T(8,128)} %fusion.10, f32[5120,256]{0,1:T(8,128)} %bitcast.95), kind=kOutput, calls=%fused_computation.12 | convolution fusion | flops 16119234560 | bytes 53497856 | tf_op jit(solution)/shard_map/dot_general | solution.py:129
  (98 shorter events, 27.1 us)
Async XLA Ops:
  7.2 95.7 %copy-start.2 = (bf16[512,1024]{1,0:T(8,128)(2,1)S(1)}, bf16[512,1024]{1,0:T(8,128)(2,1)}, u32[]{:S(2)}) copy-start(bf16[512,1024]{1,0:T(8,128)(2,1)} %param.12) | copy-start | bytes 3145732
  7.2 85.8 %all-gather.4.cloned.1.call-start = ((), (), s32[]{:S(2)}) async-start(), calls=%async_computation.4 | async-start | bytes 11141120 | tf_op jit(solution)/shard_map/all_gather | solution.py:112
  7.9 243.7 %all-gather.6.cloned.1.call-start = ((), (), s32[]{:S(2)}) async-start(), calls=%async_computation.6 | async-start | bytes 9437184 | tf_op jit(solution)/shard_map/all_gather | solution.py:11
  95.3 28.9 %copy-start.3 = (s32[32]{0:T(128)S(1)}, s32[32]{0:T(128)}, u32[]{:S(2)}) copy-start(s32[32]{0:T(128)} %param.14) | copy-start | bytes 388
  95.3 28.9 %copy-start.4 = (s32[32]{0:T(128)S(1)}, s32[32]{0:T(128)}, u32[]{:S(2)}) copy-start(s32[32]{0:T(128)} %param.13) | copy-start | bytes 388
  97.6 23.0 %all-to-all-start = ((bf16[512,16,64]{0,2,1:T(8,128)(2,1)}), bf16[512,16,64]{0,2,1:T(8,128)(2,1)S(1)}, u32[]{:S(2)}, u32[]{:S(2)}) async-start(bf16[512,16,64]{0,2,1:T(8,128)(2,1)} %bitcast.12), calls=%async_computation | async-start | bytes 2097152 | tf_op jit(solution)/shard_map/all_to_all | solution.py:81
  120.6 4.0 copy-start.1
  120.6 20.8 %all-to-all-start.2 = ((bf16[512,16,64]{0,2,1:T(8,128)(2,1)}), bf16[512,16,64]{0,2,1:T(8,128)(2,1)S(1)}, u32[]{:S(2)}, u32[]{:S(2)}) async-start(bf16[512,16,64]{0,2,1:T(8,128)(2,1)} %bitcast.16), calls=%async_computation.2 | async-start | bytes 2097152 | tf_op jit(solution)/shard_map/all_to_all | solution.py:82
  141.4 31.7 %all-to-all-start.1 = ((bf16[8,2048,64]{1,2,0:T(8,128)(2,1)}), bf16[8,2048,64]{1,2,0:T(8,128)(2,1)S(1)}, u32[]{:S(2)}, u32[]{:S(2)}) async-start(bf16[8,2048,64]{1,2,0:T(8,128)(2,1)} %copy.60), calls=%async_computation.1 | async-start | bytes 4194304 | tf_op jit(solution)/shard_map/all_to_all | solution.py:96
  173.0 35.7 %all-to-all-start.3 = ((bf16[8,2048,64]{1,2,0:T(8,128)(2,1)}), bf16[8,2048,64]{1,2,0:T(8,128)(2,1)}, u32[]{:S(2)}, u32[]{:S(2)}) async-start(bf16[8,2048,64]{1,2,0:T(8,128)(2,1)} %copy.64), calls=%async_computation.3 | async-start | bytes 4194304 | tf_op jit(solution)/shard_map/all_to_all | solution.py:97
  177.4 326.5 %all-reduce.3.cloned.1.call-start = ((), (), s32[]{:S(2)}) async-start(), calls=%async_computation.5 | async-start | bytes 2097152 | tf_op jit(solution)/shard_map/psum | solution.py:128
  388.1 7.6 %slice-start = ((s8[5242880]{0:T(1024)(128)(4,1)}), s8[4194304]{0:T(1024)(128)(4,1)S(1)}, s32[]{:S(2)}) async-start(s8[5242880]{0:T(1024)(128)(4,1)} %bitcast.97), calls=%async_computation.7 | async-start | bytes 8388608
  388.7 7.0 %slice-start.1 = ((s8[5242880]{0:T(1024)(128)(4,1)}), s8[1048576]{0:T(1024)(128)(4,1)S(1)}, s32[]{:S(2)}) async-start(s8[5242880]{0:T(1024)(128)(4,1)} %bitcast.97), calls=%async_computation.8 | async-start | bytes 2097152
  395.7 8.9 %copy-start = (f32[256,5120]{1,0:T(8,128)}, f32[256,5120]{1,0:T(8,128)S(1)}, u32[]{:S(2)}) copy-start(f32[256,5120]{1,0:T(8,128)S(1)} %fusion.4) | copy-start | bytes 15728644
Sparse Core Ops, SparseCore 0:
  10.2 82.7 all-gather.3
  95.4 49.5 all-gather.5
  439.4 64.4 all-reduce.2
